TPU v7x, 32 devices: a whole 2x2x4 slice. The times are simulated.
32 devices in a mesh: gx: 2 (over x), gy: 4 (over y, core), gz: 4 (over z).
Axes of the slice: x: 2, y: 2, z: 4, core: 2. Of those that a mesh axis runs over, the one named last changes fastest.
Arguments:
- multipoles: bfloat16 [289, 16384], P(None, ('gx', 'gy', 'gz')), may hold values from -6 to 6
- up_shift: bfloat16 [8, 289, 289], replicated, may hold values from -0.125 to 0.125
- down_shift: bfloat16 [8, 289, 289], replicated, may hold values from -0.375 to 0.375
- far_shift: bfloat16 [8, 289, 289], replicated, may hold values from -0.09375 to 0.09375
- send_list: int32 [2, 16, 16, 16], P('gx', ('gy', 'gz')), may hold values from 0 to 511
- leaf_src: int32 [16, 16384], P(None, ('gx', 'gy', 'gz')), may hold values from 0 to 767
- leaf_kind: int32 [16, 16384], P(None, ('gx', 'gy', 'gz')), may hold values from 0 to 7
- coarse_src: int32 [8, 4], replicated, may hold values from 0 to 3
- coarse_kind: int32 [8, 4], replicated, may hold values from 0 to 7
Outputs:
- leaf_local: bfloat16 [289, 16384], P(None, ('gx', 'gy', 'gz'))
All inputs are finite; a program needn't handle non-finite values.
Results may differ from a plain program's by a relative error of at most 0.014.
Values may be sent and summed in bfloat16 or wider, within the bound.
A program may use at most 128 MiB of HBM per device.

v0:
```python
import jax
import jax.numpy as jnp
from jax import lax
from jax.sharding import PartitionSpec as P

LOCAL_LEVELS = 3


def lift_level(children, up_shift):
    coefs = children.shape[0]
    count = children.shape[1] // 8
    child_stack = children.reshape(coefs, count, 8).transpose(2, 0, 1).reshape(8 * coefs, count)
    shift_table = up_shift.transpose(1, 0, 2).reshape(coefs, 8 * coefs)
    return jnp.dot(shift_table, child_stack, preferred_element_type=jnp.float32)


def lower_level(parent, down_shift):
    coefs = parent.shape[0]
    count = parent.shape[1]
    spread = jnp.dot(
        down_shift.reshape(8 * coefs, coefs), parent, preferred_element_type=jnp.float32
    )
    return spread.reshape(8, coefs, count).transpose(1, 2, 0).reshape(coefs, 8 * count)


def on_device(
    multipoles,
    up_shift,
    down_shift,
    far_shift,
    send_list,
    leaf_src,
    leaf_kind,
    coarse_src,
    coarse_kind,
):
    coefs = multipoles.shape[0]
    kind_count = far_shift.shape[0]
    flat_index = lax.axis_index(("gx", "gy", "gz"))
    coarse_box = flat_index // 8
    octant = flat_index % 8
    peer_count = lax.axis_size(("gy", "gz"))
    slot_count = send_list.shape[3]
    send_order = send_list.reshape(peer_count * slot_count)
    outgoing = jnp.take(multipoles, send_order, axis=1)
    arrived = lax.all_to_all(outgoing, ("gy", "gz"), split_axis=1, concat_axis=1, tiled=True)
    upward = multipoles
    for level in range(LOCAL_LEVELS):
        upward = lift_level(upward, up_shift).astype(jnp.bfloat16)
    every_box = lax.all_gather(upward, ("gx", "gy", "gz"), axis=1, tiled=True)
    coarse_multi = lift_level(every_box, up_shift).astype(jnp.bfloat16)
    coarse_cols = coarse_src[:, coarse_box]
    coarse_kinds = coarse_kind[:, coarse_box]
    list_len = coarse_cols.shape[0]
    coarse_picked = jnp.take(coarse_multi, coarse_cols, axis=1)
    stacked = (
        jnp.take(far_shift, coarse_kinds, axis=0)
        .transpose(1, 0, 2)
        .reshape(coefs, list_len * coefs)
    )
    column_vec = coarse_picked.transpose(1, 0).reshape(list_len * coefs, 1)
    coarse_local = jnp.dot(stacked, column_vec, preferred_element_type=jnp.float32).astype(
        jnp.bfloat16
    )
    downward = jnp.dot(down_shift[octant], coarse_local, preferred_element_type=jnp.float32).astype(
        jnp.bfloat16
    )
    for level in range(LOCAL_LEVELS - 1):
        downward = lower_level(downward, down_shift).astype(jnp.bfloat16)
    chain_part = lower_level(downward, down_shift)
    buffer = jnp.concatenate([multipoles, arrived], axis=1)
    leaf_count = leaf_src.shape[1]
    picked = jnp.take(buffer, leaf_src, axis=1)
    kind_range = jnp.arange(kind_count, dtype=jnp.int32)
    kind_hot = (leaf_kind[None, :, :] == kind_range[:, None, None]).astype(jnp.bfloat16)
    grouped = jnp.einsum("plt,klt->kpt", picked, kind_hot, preferred_element_type=jnp.float32)
    grouped = grouped.reshape(kind_count * coefs, leaf_count)
    upper_part = grouped.astype(jnp.bfloat16)
    lower_part = (grouped - upper_part.astype(jnp.float32)).astype(jnp.bfloat16)
    shift_table = far_shift.transpose(1, 0, 2).reshape(coefs, kind_count * coefs)
    far_total = jnp.dot(shift_table, upper_part, preferred_element_type=jnp.float32)
    far_total = far_total + jnp.dot(shift_table, lower_part, preferred_element_type=jnp.float32)
    return (chain_part + far_total).astype(jnp.bfloat16)


def solution(mesh):
    in_specs = (
        P(None, ("gx", "gy", "gz")),
        P(),
        P(),
        P(),
        P("gx", ("gy", "gz"), None, None),
        P(None, ("gx", "gy", "gz")),
        P(None, ("gx", "gy", "gz")),
        P(),
        P(),
    )
    out_specs = P(None, ("gx", "gy", "gz"))
    return jax.shard_map(
        on_device, mesh=mesh, in_specs=in_specs, out_specs=out_specs, check_vma=False
    )
```

profile of v0, /device:TPU:0, one launch (start us, length us, event | category | flops | bytes accessed | tf_op | source)
XLA Modules:
  0.0 177.7 jit_solution(10277228478514277687)
XLA Ops:
  0.0 0.0 copy-start.2
  0.0 0.9 reshape.143
  0.9 0.7 compare_and_fusion.1
  1.6 1.2 copy.79
  2.8 0.0 copy-start.3
  2.8 1.2 gather_fusion.2
  4.0 0.8 broadcast_select_fusion
  4.8 7.4 %all-to-all-start = ((bf16[289,16,16]{0,2,1:T(8,128)(2,1)}), bf16[289,16,16]{0,2,1:T(8,128)(2,1)}, u32[]{:S(2)}, u32[]{:S(2)}) async-start(bf16[289,16,16]{0,2,1:T(8,128)(2,1)} %broadcast_select_fusion), calls=%async_computation | async-start | bytes 393216 | tf_op jit(solution)/shard_map/all_to_all | solution.py:46
  12.3 0.7 and_bitcast_fusion.1
  13.0 1.3 and_bitcast_fusion
  14.3 0.0 copy-done.2
  14.3 3.0 %reshape.137 = bf16[289,2312]{1,0:T(8,128)(2,1)} reshape(bf16[289,8,289]{2,1,0:T(8,128)(2,1)S(1)} %bitcast.166) | data formatting | bytes 2672672 | tf_op jit(solution)/shard_map/reshape | solution.py:13
  17.2 0.0 copy-done.3
  17.2 0.7 fusion.39
  18.0 0.0 copy-start.7
  18.0 0.6 fusion.48
  18.6 0.0 copy-start
  18.6 0.1 reshape.185
  18.7 0.6 copy-done.7
  19.3 0.5 convolution_reduce_fusion.1
  19.8 68.9 %all-gather = bf16[32,1,289]{2,1,0:T(2,128)(2,1)S(1)} all-gather(bf16[1,1,289]{2,1,0:T(2,128)(2,1)S(1)} %reshape.178), channel_id=1, replica_groups=mesh['gx'=2,'gy'=4,'gz'=4] {'gx','gy','gz'}, dimensions={0}, use_global_device_ids=true | all-gather | bytes 19074 | tf_op jit(solution)/shard_map/all_gather | solution.py:50
  88.7 2.1 %fusion.57 = bf16[289,4]{0,1:T(4,128)(2,1)S(1)} fusion(bf16[289,8,289]{2,1,0:T(8,128)(2,1)} %bitcast.165, bf16[289,4,8]{0,2,1:T(8,128)(2,1)S(1)} %bitcast.174), kind=kOutput, calls=%fused_computation.42 | convolution fusion | flops 5346500 | bytes 1357144 | tf_op jit(solution)/shard_map/dot_general | solution.py:14
  90.8 0.0 copy-done
  90.8 6.9 %gather_fusion = bf16[8,289,289]{2,0,1:T(8,128)(2,1)} fusion(bf16[8,289,289]{2,0,1:T(8,128)(2,1)S(1)} %copy-done, s32[1024]{0:T(1024)S(1)} %pad_clamp_fusion.2), kind=kCustom, calls=%fused_computation | custom fusion | bytes 2672704 | tf_op jit(solution)/shard_map/jit(_take)/gather | solution.py:57
  97.6 3.0 %select_bitcast_fusion = bf16[289,8,289]{2,1,0:T(8,128)(2,1)} fusion(bf16[8,289,289]{2,0,1:T(8,128)(2,1)} %gather_fusion, pred[8]{0:T(512)(128)(4,1)S(1)} %get-tuple-element.7), kind=kLoop, calls=%fused_computation.21 | loop fusion | flops 668168 | bytes 2672680 | tf_op jit(solution)/shard_map/jit(_take)/select_n | solution.py:57
  100.7 1.2 gather_fusion.1
  101.8 0.0 copy-start.5
  101.8 0.9 select_bitcast_fusion.1
  102.7 2.1 %fusion.60 = bf16[289]{0:T(512)(128)(2,1)S(1)} fusion(bf16[289,8,289]{2,1,0:T(8,128)(2,1)} %select_bitcast_fusion, bf16[8,289,1]{1,0,2:T(8,128)(2,1)S(1)} %select_bitcast_fusion.1), kind=kOutput, calls=%fused_computation.43 | convolution fusion | flops 1336336 | bytes 1341538 | tf_op jit(solution)/shard_map/dot_general | solution.py:62
  104.8 0.6 reshape.190
  105.4 0.0 copy-done.5
  105.4 3.1 %copy.86 = bf16[8,289,289]{1,0,2:T(8,128)(2,1)} copy(bf16[8,289,289]{2,0,1:T(8,128)(2,1)S(1)} %copy-done.5) | data formatting | bytes 2672672 | tf_op args[2]
  108.5 0.5 constant_dynamic-slice_fusion.2
  109.0 0.9 convolution_reduce_fusion
  109.9 1.3 fusion.8
  111.2 0.0 copy-start.10
  111.2 3.3 %reshape.139 = bf16[2312,289]{0,1:T(8,128)(2,1)S(1)} reshape(bf16[8,289,289]{1,0,2:T(8,128)(2,1)} %copy.86) | data formatting | bytes 2672672 | tf_op jit(solution)/shard_map/reshape | solution.py:21
  114.4 0.0 copy-done.10
  114.4 0.0 copy-start.8
  114.4 0.3 fusion.4
  114.8 0.1 convert_element_type.88
  114.9 1.2 convolution_bitcast_fusion
  116.1 0.0 copy-done.8
  116.1 0.0 copy-start.9
  116.2 1.5 reshape.140
  117.7 0.2 copy.97
  118.0 0.0 copy-done.9
  118.0 0.1 copy.87
  118.1 0.2 copy.88
  118.3 0.0 copy-start.4
  118.3 3.2 %copy.103 = bf16[289,8,289]{0,1,2:T(8,128)(2,1)} copy(bf16[289,8,289]{2,1,0:T(8,128)(2,1)S(1)} %bitcast.164) | data formatting | bytes 2672672 | tf_op jit(solution)/shard_map/transpose | solution.py:80
  121.4 0.0 all-to-all-done
  121.5 0.0 copy-done.4
  121.5 1.0 pad_maximum_fusion
  122.5 33.3 %gather_fusion.3 = bf16[8192,289]{1,0:T(8,128)(2,1)} fusion(bf16[289,768]{0,1:T(8,128)(2,1)S(1)} %pad_maximum_fusion, s32[8192]{0:T(1024)S(1)} %broadcast_clamp_fusion), kind=kCustom, calls=%fused_computation.3 | custom fusion | bytes 9502720 | tf_op jit(solution)/shard_map/jit(_take)/gather | solution.py:73
  155.8 9.9 %fusion = f32[512,8,289]{2,1,0:T(8,128)} fusion(bf16[16,512,289]{2,1,0:T(8,128)(2,1)} %bitcast.170, pred[16,512]{0,1:T(8,128)(4,1)S(1)} %copy.88, s32[16,512]{0,1:T(8,128)S(1)} %copy.87), kind=kOutput, calls=%fused_computation.4 | convolution fusion | flops 40312832 | bytes 9510912 | tf_op jit(solution)/shard_map/plt,klt->kpt/dot_general | solution.py:76
  165.7 0.0 copy-start.6
  165.7 6.5 %copy.92 = f32[512,8,289]{0,1,2:T(8,128)} copy(f32[512,8,289]{2,1,0:T(8,128)} %fusion) | data formatting | bytes 9469952 | tf_op jit(solution)/shard_map/plt,klt->kpt/dot_general | solution.py:76
  172.2 0.0 copy-done.6
  172.2 0.0 copy-start.1
  172.2 3.5 %convolution_bitcast_fusion.1 = f32[512,289]{0,1:T(8,128)S(1)} fusion(bf16[289,8,289]{0,1,2:T(8,128)(2,1)S(1)} %copy-done.6, f32[512,8,289]{0,1,2:T(8,128)} %copy.92), kind=kOutput, calls=%fused_computation.29 | convolution fusion | flops 684204032 | bytes 6663184 | tf_op jit(solution)/shard_map/dot_general | solution.py:81
  175.7 0.2 copy-done.1
  176.0 1.7 fusion.30
  (11 shorter events, 0.1 us)
Async XLA Ops:
  0.0 14.3 %copy-start.2 = (bf16[8,289,289]{2,0,1:T(8,128)(2,1)S(1)}, bf16[8,289,289]{2,0,1:T(8,128)(2,1)}, u32[]{:S(2)}) copy-start(bf16[8,289,289]{2,0,1:T(8,128)(2,1)} %param.10) | copy-start | bytes 4009012
  2.8 14.4 %copy-start.3 = (bf16[289,512]{0,1:T(8,128)(2,1)}, bf16[289,512]{0,1:T(8,128)(2,1)S(1)}, u32[]{:S(2)}) copy-start(bf16[289,512]{0,1:T(8,128)(2,1)S(1)} %copy.79) | copy-start | bytes 887812
  4.8 116.7 %all-to-all-start = ((bf16[289,16,16]{0,2,1:T(8,128)(2,1)}), bf16[289,16,16]{0,2,1:T(8,128)(2,1)}, u32[]{:S(2)}, u32[]{:S(2)}) async-start(bf16[289,16,16]{0,2,1:T(8,128)(2,1)} %broadcast_select_fusion), calls=%async_computation | async-start | bytes 393216 | tf_op jit(solution)/shard_map/all_to_all | solution.py:46
  18.0 1.4 copy-start.7
  18.6 72.2 %copy-start = (bf16[8,289,289]{2,0,1:T(8,128)(2,1)S(1)}, bf16[8,289,289]{2,0,1:T(8,128)(2,1)}, u32[]{:S(2)}) copy-start(bf16[8,289,289]{2,0,1:T(8,128)(2,1)} %param.12) | copy-start | bytes 4009012
  101.8 3.6 %copy-start.5 = (bf16[8,289,289]{2,0,1:T(8,128)(2,1)S(1)}, bf16[8,289,289]{2,0,1:T(8,128)(2,1)}, u32[]{:S(2)}) copy-start(bf16[8,289,289]{2,0,1:T(8,128)(2,1)} %param.11) | copy-start | bytes 4009012
  111.2 3.3 %copy-start.10 = (bf16[1,8,289]{2,0,1:T(2,128)(2,1)S(1)}, bf16[1,8,289]{2,0,1:T(2,128)(2,1)}, u32[]{:S(2)}) copy-start(bf16[1,8,289]{2,0,1:T(2,128)(2,1)} %fusion.8) | copy-start | bytes 13876
  114.4 1.7 copy-start.8
  116.1 1.8 %copy-start.9 = (s32[16,512]{1,0:T(8,128)S(1)}, s32[16,512]{1,0:T(8,128)}, u32[]{:S(2)}) copy-start(s32[16,512]{1,0:T(8,128)} %param.15) | copy-start | bytes 98308
  118.3 3.2 %copy-start.4 = (bf16[289,512]{0,1:T(8,128)(2,1)S(1)}, bf16[289,512]{0,1:T(8,128)(2,1)}, u32[]{:S(2)}) copy-start(bf16[289,512]{0,1:T(8,128)(2,1)} %copy-done.3) | copy-start | bytes 887812
  165.7 6.5 %copy-start.6 = (bf16[289,8,289]{0,1,2:T(8,128)(2,1)S(1)}, bf16[289,8,289]{0,1,2:T(8,128)(2,1)}, u32[]{:S(2)}) copy-start(bf16[289,8,289]{0,1,2:T(8,128)(2,1)} %copy.103) | copy-start | bytes 4009012
  172.2 3.8 %copy-start.1 = (f32[512,8,289]{0,1,2:T(8,128)S(1)}, f32[512,8,289]{0,1,2:T(8,128)}, u32[]{:S(2)}) copy-start(f32[512,8,289]{0,1,2:T(8,128)} %copy.92) | copy-start | bytes 14204932
where the time goes:
time: 178 us
  blocking collectives  68.9 us (39%)
  local copies, waits for them, and re-layouts  67.8 us (38%)
  matrix products  24.9 us (14%)
  other arithmetic  8.46 us (5%)
  starting transfers between devices  7.43 us (4%)
    all_gather x1, blocking collectives, on_device(): every_box = lax.all_gather(upward, ('gx', 'gy', 'gz'), axis=1, tiled=True)  68.9 us
    gather x1, local copies, waits for them, and re-layouts, on_device(): picked = jnp.take(buffer, leaf_src, axis=1)  33.3 us
    dot_general x1, matrix products, on_device(): jnp.einsum('plt,klt->kpt', picked, kind_hot, preferred_element_type=jnp.f...  9.95 us
    all_to_all x1, starting transfers between devices, on_device(): lax.all_to_all(outgoing, ('gy', 'gz'), split_axis=1, concat_axis=1, tiled...  7.43 us
    gather x1, local copies, waits for them, and re-layouts, on_device(): jnp.take(far_shift, coarse_kinds, axis=0).transpose(1, 0, 2)  6.86 us
    dot_general x1, local copies, waits for them, and re-layouts, on_device(): jnp.einsum('plt,klt->kpt', picked, kind_hot, preferred_element_type=jnp.f...  6.48 us
    unnamed x28, local copies, waits for them, and re-layouts  5.34 us
    dot_general x4, matrix products, lift_level(): return jnp.dot(shift_table, child_stack, preferred_element_type=jnp.float32)  3.87 us
  transfers between devices with their start and end apart: 1, of which 0 were waited for; matrix products, arithmetic and copies ran while one was open for 22% of the time, Pallas kernels for 0%

commit v1 on v0

v1 whole, which is shorter than its diff:
```python
import functools

import jax
import jax.numpy as jnp
from jax import lax
from jax.experimental import pallas as pl
from jax.experimental.pallas import tpu as pltpu
from jax.sharding import PartitionSpec as P

MESH = pl.DeviceIdType.MESH
LOCAL_LEVELS = 3
LANES = 128
ROWS = 64
FIELD = 15
LOW_NIBBLES = 0x0F0F0F0F
F32 = jnp.float32
BF16 = jnp.bfloat16


def iota(shape, dim):
    return lax.broadcasted_iota(jnp.int32, shape, dim)


def dot(a, b):
    return jnp.dot(a, b, preferred_element_type=F32)


def pick_children(rows):
    shape = (rows, 8 * LANES)
    col = iota(shape, 1)
    return (iota(shape, 0) == 8 * (col % LANES) + col // LANES).astype(F32).astype(BF16)


def spread_children():
    shape = (LANES, 8 * LANES)
    col = iota(shape, 1)
    place = col % LANES
    hit = (iota(shape, 0) == place // 8) & (place % 8 == col // LANES)
    return hit.astype(F32).astype(BF16)


def apply_eight(table, blocks):
    total = None
    for c in range(8):
        term = dot(table(c), blocks[:, c * LANES : (c + 1) * LANES])
        total = term if total is None else total + term
    return total


def kernel(
    sizes,
    mult_hbm,
    up_hbm,
    down_hbm,
    far_hbm,
    send_ref,
    src_ref,
    kind_ref,
    csrc_ref,
    ckind_ref,
    out_ref,
    mult,
    up,
    down,
    farw,
    sel,
    spread,
    out_rows,
    arrived,
    table,
    buf,
    far_total,
    turn,
    message,
    boxes,
    load_sem,
    a2a_send,
    a2a_recv,
    box_send,
    box_recv,
):
    n_gx, n_gy, n_gz = sizes
    peers = n_gy * n_gz
    devices = n_gx * peers
    gx = lax.axis_index("gx")
    q = lax.axis_index("gy") * n_gz + lax.axis_index("gz")
    me = gx * peers + q
    coefs, leaves = mult.shape
    slots = send_ref.shape[1]
    kinds = farw.shape[0]
    sources = table.shape[1]
    list_len = src_ref.shape[0]

    loads = [
        pltpu.make_async_copy(a, b, load_sem.at[i])
        for i, (a, b) in enumerate(
            ((mult_hbm, mult), (up_hbm, up), (far_hbm, farw), (down_hbm, down))
        )
    ]
    for load in loads:
        load.start()

    def device_of(flat):
        return (flat // peers, (flat % peers) // n_gz, flat % n_gz)

    barrier = pltpu.get_barrier_semaphore()

    def greet(i, carry):
        pl.semaphore_signal(
            barrier, inc=1, device_id=device_of((me + i) % devices), device_id_type=MESH
        )
        return carry

    lax.fori_loop(1, devices, greet, 0)

    count = peers * slots
    row_of = (iota((count, peers), 0) // slots == iota((count, peers), 1)).astype(F32).astype(BF16)
    wanted = send_ref[...]
    upper = dot(row_of, (wanted // 32).astype(F32).astype(BF16))
    lower = dot(row_of, (wanted % 32).astype(F32).astype(BF16))
    mine = iota((count, slots), 0) % slots == iota((count, slots), 1)
    leaf = jnp.sum(jnp.where(mine, upper * 32.0 + lower, 0.0), axis=1, keepdims=True)
    hot = (leaf.astype(jnp.int32) == iota((count, leaves), 1)).astype(F32).astype(BF16)
    sel[...] = pick_children(leaves)
    spread[...] = spread_children()
    out_rows[...] = jnp.zeros_like(out_rows)
    loads[0].wait()
    out_rows[:, :coefs] = lax.dot_general(
        hot, mult[...], (((1,), (1,)), ((), ())), preferred_element_type=F32
    ).astype(BF16)
    own = pl.ds(pl.multiple_of(q * slots, slots), slots)
    arrived[own, :] = out_rows[own, :]

    pl.semaphore_wait(barrier, devices - 1)

    def send_rows(i, carry):
        other = (q + i) % peers
        pltpu.make_async_remote_copy(
            src_ref=out_rows.at[pl.ds(pl.multiple_of(other * slots, slots), slots)],
            dst_ref=arrived.at[own],
            send_sem=a2a_send,
            recv_sem=a2a_recv,
            device_id=(gx, other // n_gz, other % n_gz),
            device_id_type=MESH,
        ).start()
        return carry

    lax.fori_loop(1, peers, send_rows, 0)

    loads[1].wait()
    turn[...] = jnp.zeros_like(turn)
    x = mult[...]
    for level in range(LOCAL_LEVELS):
        picked = dot(x, sel[: x.shape[1], :]).astype(BF16)
        total = apply_eight(lambda c: up[c], picked)
        x = total.astype(BF16)
    turn[:coefs, :] = x.astype(F32)
    row = turn[...].T[0:1, :]
    message[...] = row
    boxes[me] = row

    def send_box(i, carry):
        pltpu.make_async_remote_copy(
            src_ref=message,
            dst_ref=boxes.at[me],
            send_sem=box_send,
            recv_sem=box_recv,
            device_id=device_of((me + i) % devices),
            device_id_type=MESH,
        ).start()
        return carry

    lax.fori_loop(1, devices, send_box, 0)

    def count_rows(step, carry):
        s0 = pl.multiple_of(step * ROWS, ROWS)
        for lane in range(0, leaves, LANES):
            cols = slice(lane, lane + LANES)
            sid = iota((ROWS, LANES), 0) + s0
            parts = []
            for start in range(0, list_len, FIELD):
                acc = jnp.zeros((ROWS, LANES), jnp.int32)
                for j in range(start, min(start + FIELD, list_len)):
                    weight = lax.shift_left(jnp.int32(1), 4 * kind_ref[j : j + 1, cols])
                    acc = acc + jnp.where(src_ref[j : j + 1, cols] == sid, weight, 0)
                parts.append(acc)
            even = sum(a & LOW_NIBBLES for a in parts)
            odd = sum(lax.shift_right_logical(a, 4) & LOW_NIBBLES for a in parts)
            for k in range(kinds):
                word = odd if k % 2 else even
                field = lax.shift_right_logical(word, 8 * (k // 2)) & 255
                table[k, pl.ds(s0, ROWS), cols] = field.astype(F32).astype(BF16)
        return carry

    lax.fori_loop(0, sources // ROWS, count_rows, 0)

    buf[:, :leaves] = mult[...]
    part = arrived.at[pl.ds(0, (peers - 1) * slots)]
    pltpu.make_async_copy(part, part, a2a_recv).wait()
    buf[:, leaves:] = arrived[...].astype(F32).T[:coefs, :].astype(BF16)
    loads[2].wait()
    far_total[...] = jnp.zeros_like(far_total)

    def add_kind(k, carry):
        grouped = dot(buf[...], table[k]).astype(BF16)
        far_total[...] += dot(farw[k], grouped)
        return carry

    lax.fori_loop(0, kinds, add_kind, 0)

    part = boxes.at[pl.ds(0, devices - 1)]
    pltpu.make_async_copy(part, part, box_recv).wait()
    x = boxes[...].reshape(devices, boxes.shape[2]).T[:coefs, :].astype(BF16)
    picked = dot(x, sel[:devices, :]).astype(BF16)
    coarse = apply_eight(lambda c: up[c], picked).astype(BF16)
    box = me // 8
    total = None
    for j in range(csrc_ref.shape[0]):
        hit = (iota((LANES, LANES), 0) == csrc_ref[j, box]) & (iota((LANES, LANES), 1) == 0)
        picked = dot(coarse, hit.astype(F32).astype(BF16)).astype(BF16)
        term = dot(farw[ckind_ref[j, box]], picked)
        total = term if total is None else total + term
    x = total.astype(BF16)

    loads[3].wait()
    x = dot(down[me % 8], x).astype(BF16)
    for level in range(LOCAL_LEVELS - 1):
        picked = dot(x, spread[...]).astype(BF16)
        x = apply_eight(lambda c: down[c], picked).astype(BF16)
    half = LANES // 2
    shape = (LANES, LANES)
    shift = ((iota(shape, 0) + half == iota(shape, 1)) & (iota(shape, 0) < half)).astype(F32)
    shifted = dot(x, shift.astype(BF16)).astype(BF16)
    result = far_total[...]
    for pair in range(4):
        chain = dot(down[2 * pair], x) + dot(down[2 * pair + 1], shifted)
        upper = chain.astype(BF16)
        lower = (chain - upper.astype(F32)).astype(BF16)
        place = iota((LANES, leaves), 0)
        goes = 8 * (place % half) + place // half + 2 * pair
        spot = (goes == iota((LANES, leaves), 1)).astype(F32).astype(BF16)
        result = result + dot(upper, spot) + dot(lower, spot)
    out_ref[...] = result.astype(BF16)

    part = out_rows.at[pl.ds(0, (peers - 1) * slots)]
    pltpu.make_async_copy(part, part, a2a_send).wait()
    part = boxes.at[pl.ds(0, devices - 1)]
    pltpu.make_async_copy(part, part, box_send).wait()


def solution(mesh):
    sizes = (mesh.shape["gx"], mesh.shape["gy"], mesh.shape["gz"])
    peers = sizes[1] * sizes[2]
    devices = sizes[0] * peers

    def on_device(mult, up, down, farw, send, src, kind, csrc, ckind):
        coefs, leaves = mult.shape
        kinds = farw.shape[0]
        slots = send.shape[3]
        sources = leaves + peers * slots
        wide = -(-coefs // LANES) * LANES
        vmem = pl.BlockSpec(memory_space=pltpu.VMEM)
        smem = pl.BlockSpec(memory_space=pltpu.SMEM)
        hbm = pl.BlockSpec(memory_space=pl.ANY)
        return pl.pallas_call(
            functools.partial(kernel, sizes),
            out_shape=jax.ShapeDtypeStruct((coefs, leaves), BF16),
            in_specs=[hbm] * 4 + [vmem] * 3 + [smem] * 2,
            out_specs=vmem,
            scratch_shapes=[
                pltpu.VMEM(mult.shape, BF16),
                pltpu.VMEM(up.shape, BF16),
                pltpu.VMEM(down.shape, BF16),
                pltpu.VMEM(farw.shape, BF16),
                pltpu.VMEM((leaves, 8 * LANES), BF16),
                pltpu.VMEM((LANES, 8 * LANES), BF16),
                pltpu.VMEM((peers * slots, wide), BF16),
                pltpu.VMEM((peers * slots, wide), BF16),
                pltpu.VMEM((kinds, sources, leaves), BF16),
                pltpu.VMEM((coefs, sources), BF16),
                pltpu.VMEM((coefs, leaves), F32),
                pltpu.VMEM((wide, LANES), F32),
                pltpu.VMEM((1, wide), F32),
                pltpu.VMEM((devices, 1, wide), F32),
                pltpu.SemaphoreType.DMA((4,)),
                pltpu.SemaphoreType.DMA,
                pltpu.SemaphoreType.DMA,
                pltpu.SemaphoreType.DMA,
                pltpu.SemaphoreType.DMA,
            ],
            compiler_params=pltpu.CompilerParams(
                collective_id=0, has_side_effects=True, vmem_limit_bytes=50 * 2**20
            ),
        )(mult, up, down, farw, send.reshape(peers, slots), src, kind, csrc, ckind)

    leaf = P(None, ("gx", "gy", "gz"))
    in_specs = (leaf, P(), P(), P(), P("gx", ("gy", "gz"), None, None), leaf, leaf, P(), P())
    return jax.shard_map(
        on_device, mesh=mesh, in_specs=in_specs, out_specs=leaf, check_vma=False
    )
```

time: 178 us -> 42.1 us (0.24)
  blocking collectives: 68.9 us -> 0 us
  local copies, waits for them, and re-layouts: 67.8 us -> 7.68 us
  Pallas kernels: 0 us -> 34.2 us
  matrix products: 24.9 us -> 0 us
  other arithmetic: 8.46 us -> 0 us
  starting transfers between devices: 7.43 us -> 0 us
    all_gather x1 -> x0, blocking collectives: 68.9 us -> none  [on_device(): every_box = lax.all_gather(upward, ('gx', 'gy', 'gz'), axis=1, tiled=True)]
    gather x4 -> x0, local copies, waits for them, and re-layouts: 42.5 us -> none  [the longest x1 33.3 us: on_device(): picked = jnp.take(buffer, leaf_src, axis=1)]
    pallas_call x0 -> x1, Pallas kernels: none -> 34.2 us  [on_device(): pl.pallas_call(functools.partial(kernel, sizes), out_shape=jax.ShapeDtype...]
    dot_general x12 -> x0, matrix products: 24.9 us -> none  [the longest x1 9.95 us: on_device(): jnp.einsum('plt,klt->kpt', picked, kind_hot, preferred_element_type=jnp.f...]
    reshape x5 -> x0, local copies, waits for them, and re-layouts: 8.87 us -> none  [the longest x1 3.25 us: lower_level(): down_shift.reshape(8 * coefs, coefs)]
    all_to_all x1 -> x0, starting transfers between devices: 7.43 us -> none  [on_device(): lax.all_to_all(outgoing, ('gy', 'gz'), split_axis=1, concat_axis=1, tiled...]
    dot_general x1 -> x0, local copies, waits for them, and re-layouts: 6.48 us -> none  [on_device(): jnp.einsum('plt,klt->kpt', picked, kind_hot, preferred_element_type=jnp.f...]
    select_n x4 -> x0, other arithmetic: 4.73 us -> none  [the longest x1 3.04 us: on_device(): jnp.take(far_shift, coarse_kinds, axis=0).transpose(1, 0, 2)]
  transfers between devices with their start and end apart: 1 -> 0, of which waited for: 0 -> 0; matrix products, arithmetic and copies ran while one was open for 22% -> 0% of each run, Pallas kernels for 0% -> 0%
where the time goes in v1:
time: 42.1 us; the launch traced here: 41.9 us
  Pallas kernels  34.2 us (81%)
  local copies, waits for them, and re-layouts  7.68 us (18%)
    pallas_call x1, Pallas kernels, on_device(): pl.pallas_call(functools.partial(kernel, sizes), out_shape=jax.ShapeDtype...  34.2 us
    unnamed x18, local copies, waits for them, and re-layouts  7.68 us

profile of v1, /device:TPU:0, one launch (start us, length us, event | category | flops | bytes accessed | tf_op | source)
XLA Modules:
  0.0 41.9 jit_solution(9268127793581167586)
XLA Ops:
  0.0 0.0 copy-start.4
  0.0 0.9 %copy.13.csrc_ref = s32[8,4]{1,0:T(8,128)S(1)} copy(s32[8,4]{0,1:T(4,128)} %param.16) | data formatting | bytes 256 | tf_op args[7]
  0.9 0.8 %copy.14.ckind_ref = s32[8,4]{1,0:T(8,128)S(1)} copy(s32[8,4]{0,1:T(4,128)} %param.17) | data formatting | bytes 256 | tf_op args[8]
  1.6 1.7 %copy.10.up_hbm = bf16[8,289,289]{2,1,0:T(8,128)(2,1)S(1)} copy(bf16[8,289,289]{2,0,1:T(8,128)(2,1)} %param.10) | data formatting | bytes 2672672 | tf_op args[1]
  3.4 0.0 copy-done.4
  3.4 0.0 copy-start.5
  3.4 1.5 %copy.11.down_hbm = bf16[8,289,289]{2,1,0:T(8,128)(2,1)} copy(bf16[8,289,289]{2,0,1:T(8,128)(2,1)S(1)} %copy-done.4) | data formatting | bytes 2672672 | tf_op args[2]
  4.9 0.6 %copy-done.5 = bf16[8,289,289]{2,0,1:T(8,128)(2,1)S(1)} copy-done((bf16[8,289,289]{2,0,1:T(8,128)(2,1)S(1)}, bf16[8,289,289]{2,0,1:T(8,128)(2,1)}, u32[]{:S(2)}) %copy-start.5) | copy-done | bytes 1336360
  5.5 0.0 copy-start
  5.5 0.0 copy-start.1
  5.5 0.0 copy-start.2
  5.5 0.0 copy-start.3
  5.5 1.5 %copy.12.far_hbm = bf16[8,289,289]{2,1,0:T(8,128)(2,1)} copy(bf16[8,289,289]{2,0,1:T(8,128)(2,1)S(1)} %copy-done.5) | data formatting | bytes 2672672 | tf_op args[3]
  7.0 0.0 copy-done
  7.0 0.0 copy-done.1
  7.0 0.0 copy-done.2
  7.0 0.0 copy-done.3
  7.0 34.2 %shard_map.91 = bf16[289,512]{1,0:T(8,128)(2,1)S(1)} custom-call(bf16[289,512]{1,0:T(8,128)(2,1)S(1)} %copy-done, bf16[8,289,289]{2,1,0:T(8,128)(2,1)S(1)} %copy.10.up_hbm, bf16[8,289,289]{2,1,0:T(8,128)(2,1)} %copy.11.down_hbm, bf16[8,289,289]{2,1,0:T(8,128)(2,1)} %copy.12.far_hbm, s32[16,16]{1,0:T(8,128)S(1)} %bitcast.1, s32[16,512]{1,0:T(8,128)S(1)} %copy-done.1, ...), custom_call_target="tpu_custom_call" | custom-call | tf_op jit(solution)/shard_map/pallas_call | solution.py:265
  41.2 0.7 %copy.16 = bf16[289,512]{1,0:T(8,128)(2,1)} copy(bf16[289,512]{1,0:T(8,128)(2,1)S(1)} %shard_map.91) | data formatting | bytes 591872
Async XLA Ops:
  0.0 3.4 %copy-start.4 = (bf16[8,289,289]{2,0,1:T(8,128)(2,1)S(1)}, bf16[8,289,289]{2,0,1:T(8,128)(2,1)}, u32[]{:S(2)}) copy-start(bf16[8,289,289]{2,0,1:T(8,128)(2,1)} %param.11) | copy-start | bytes 4009012
  3.4 2.1 %copy-start.5 = (bf16[8,289,289]{2,0,1:T(8,128)(2,1)S(1)}, bf16[8,289,289]{2,0,1:T(8,128)(2,1)}, u32[]{:S(2)}) copy-start(bf16[8,289,289]{2,0,1:T(8,128)(2,1)} %param.12) | copy-start | bytes 4009012
  5.5 1.5 %copy-start = (bf16[289,512]{1,0:T(8,128)(2,1)S(1)}, bf16[289,512]{1,0:T(8,128)(2,1)}, u32[]{:S(2)}) copy-start(bf16[289,512]{1,0:T(8,128)(2,1)} %mult_hbm.1) | copy-start | bytes 887812
  5.5 1.5 %copy-start.1 = (s32[16,512]{1,0:T(8,128)S(1)}, s32[16,512]{1,0:T(8,128)}, u32[]{:S(2)}) copy-start(s32[16,512]{1,0:T(8,128)} %src_ref.1) | copy-start | bytes 98308
  5.5 1.5 %copy-start.2 = (s32[16,512]{1,0:T(8,128)S(1)}, s32[16,512]{1,0:T(8,128)}, u32[]{:S(2)}) copy-start(s32[16,512]{1,0:T(8,128)} %kind_ref.1) | copy-start | bytes 98308
  5.5 1.5 %copy-start.3 = (s32[1,1,16,16]{3,2,1,0:T(8,128)S(1)}, s32[1,1,16,16]{3,2,1,0:T(8,128)}, u32[]{:S(2)}) copy-start(s32[1,1,16,16]{3,2,1,0:T(8,128)} %param.13) | copy-start | bytes 3076

commit v2 on v1

--- a/solution.py
+++ b/solution.py
@@ -11,6 +11,7 @@
 LOCAL_LEVELS = 3
 LANES = 128
 ROWS = 64
+BLOCK = 32
 FIELD = 15
 LOW_NIBBLES = 0x0F0F0F0F
 F32 = jnp.float32
@@ -45,6 +46,30 @@
         term = dot(table(c), blocks[:, c * LANES : (c + 1) * LANES])
         total = term if total is None else total + term
     return total
+
+
+def split_octants(raw, table, step):
+    shape = (8 * BLOCK, 8 * BLOCK)
+    to, frm = iota(shape, 0), iota(shape, 1)
+    order = (frm == 8 * (to % BLOCK) + to // BLOCK).astype(F32).astype(BF16)
+    rows = raw[pl.ds(pl.multiple_of(step * 8 * BLOCK, 8 * BLOCK), 8 * BLOCK), :]
+    out = dot(order, rows).astype(BF16)
+    for c in range(8):
+        spot = pl.ds(pl.multiple_of(step * BLOCK, BLOCK), BLOCK)
+        table[c, spot, :] = out[c * BLOCK : (c + 1) * BLOCK]
+
+
+def split_tail(raw, table):
+    coefs = raw.shape[0] // 8
+    done = coefs // BLOCK * BLOCK
+    left = coefs - done
+    room = table.shape[1] - done
+    shape = (8 * room, 8 * left)
+    to, frm = iota(shape, 0), iota(shape, 1)
+    hit = (frm == 8 * (to % room) + to // room) & (to % room < left)
+    out = dot(hit.astype(F32).astype(BF16), raw[8 * done :, :]).astype(BF16)
+    for c in range(8):
+        table[c, done:, :] = out[c * room : (c + 1) * room]
 
 
 def kernel(
@@ -60,6 +85,9 @@
     ckind_ref,
     out_ref,
     mult,
+    up_raw,
+    down_raw,
+    far_raw,
     up,
     down,
     farw,
@@ -94,7 +122,7 @@
     loads = [
         pltpu.make_async_copy(a, b, load_sem.at[i])
         for i, (a, b) in enumerate(
-            ((mult_hbm, mult), (up_hbm, up), (far_hbm, farw), (down_hbm, down))
+            ((up_hbm, up_raw), (mult_hbm, mult), (far_hbm, far_raw), (down_hbm, down_raw))
         )
     ]
     for load in loads:
@@ -112,6 +140,29 @@
         return carry
 
     lax.fori_loop(1, devices, greet, 0)
+
+    sel[...] = pick_children(leaves)
+    spread[...] = spread_children()
+    blocks = coefs // BLOCK
+    loads[0].wait()
+
+    def split_up(i, carry):
+        split_octants(up_raw, up, i)
+        return carry
+
+    lax.fori_loop(0, blocks, split_up, 0)
+    split_tail(up_raw, up)
+    loads[1].wait()
+    turn[...] = jnp.zeros_like(turn)
+    x = mult[...]
+    for level in range(LOCAL_LEVELS):
+        picked = dot(x, sel[: x.shape[1], :]).astype(BF16)
+        total = apply_eight(lambda c: up[c, :coefs, :], picked)
+        x = total.astype(BF16)
+    turn[:coefs, :] = x.astype(F32)
+    row = turn[...].T[0:1, :]
+    message[...] = row
+    boxes[me] = row
 
     count = peers * slots
     row_of = (iota((count, peers), 0) // slots == iota((count, peers), 1)).astype(F32).astype(BF16)
@@ -121,10 +172,7 @@
     mine = iota((count, slots), 0) % slots == iota((count, slots), 1)
     leaf = jnp.sum(jnp.where(mine, upper * 32.0 + lower, 0.0), axis=1, keepdims=True)
     hot = (leaf.astype(jnp.int32) == iota((count, leaves), 1)).astype(F32).astype(BF16)
-    sel[...] = pick_children(leaves)
-    spread[...] = spread_children()
     out_rows[...] = jnp.zeros_like(out_rows)
-    loads[0].wait()
     out_rows[:, :coefs] = lax.dot_general(
         hot, mult[...], (((1,), (1,)), ((), ())), preferred_element_type=F32
     ).astype(BF16)
@@ -132,6 +180,19 @@
     arrived[own, :] = out_rows[own, :]
 
     pl.semaphore_wait(barrier, devices - 1)
+
+    def send_box(i, carry):
+        pltpu.make_async_remote_copy(
+            src_ref=message,
+            dst_ref=boxes.at[me],
+            send_sem=box_send,
+            recv_sem=box_recv,
+            device_id=device_of((me + i) % devices),
+            device_id_type=MESH,
+        ).start()
+        return carry
+
+    lax.fori_loop(1, devices, send_box, 0)
 
     def send_rows(i, carry):
         other = (q + i) % peers
@@ -146,31 +207,6 @@
         return carry
 
     lax.fori_loop(1, peers, send_rows, 0)
-
-    loads[1].wait()
-    turn[...] = jnp.zeros_like(turn)
-    x = mult[...]
-    for level in range(LOCAL_LEVELS):
-        picked = dot(x, sel[: x.shape[1], :]).astype(BF16)
-        total = apply_eight(lambda c: up[c], picked)
-        x = total.astype(BF16)
-    turn[:coefs, :] = x.astype(F32)
-    row = turn[...].T[0:1, :]
-    message[...] = row
-    boxes[me] = row
-
-    def send_box(i, carry):
-        pltpu.make_async_remote_copy(
-            src_ref=message,
-            dst_ref=boxes.at[me],
-            send_sem=box_send,
-            recv_sem=box_recv,
-            device_id=device_of((me + i) % devices),
-            device_id_type=MESH,
-        ).start()
-        return carry
-
-    lax.fori_loop(1, devices, send_box, 0)
 
     def count_rows(step, carry):
         s0 = pl.multiple_of(step * ROWS, ROWS)
@@ -192,48 +228,61 @@
                 table[k, pl.ds(s0, ROWS), cols] = field.astype(F32).astype(BF16)
         return carry
 
-    lax.fori_loop(0, sources // ROWS, count_rows, 0)
+    def count_and_split(step, carry):
+        split_octants(far_raw, farw, step)
+        split_octants(down_raw, down, step)
+        return count_rows(step, carry)
+
+    loads[2].wait()
+    loads[3].wait()
+    both = min(blocks, sources // ROWS)
+    assert both == blocks
+    lax.fori_loop(0, both, count_and_split, 0)
+    lax.fori_loop(both, sources // ROWS, count_rows, 0)
+    split_tail(far_raw, farw)
+    split_tail(down_raw, down)
 
     buf[:, :leaves] = mult[...]
     part = arrived.at[pl.ds(0, (peers - 1) * slots)]
     pltpu.make_async_copy(part, part, a2a_recv).wait()
     buf[:, leaves:] = arrived[...].astype(F32).T[:coefs, :].astype(BF16)
-    loads[2].wait()
-    far_total[...] = jnp.zeros_like(far_total)
-
-    def add_kind(k, carry):
-        grouped = dot(buf[...], table[k]).astype(BF16)
-        far_total[...] += dot(farw[k], grouped)
-        return carry
-
-    lax.fori_loop(0, kinds, add_kind, 0)
-
     part = boxes.at[pl.ds(0, devices - 1)]
     pltpu.make_async_copy(part, part, box_recv).wait()
+    far_total[...] = jnp.zeros_like(far_total)
+
+    def add_kinds(which):
+        for k in which:
+            grouped = dot(buf[...], table[k]).astype(BF16)
+            far_total[...] += dot(farw[k, :coefs, :], grouped)
+
+    turns = [range(t * kinds // 4, (t + 1) * kinds // 4) for t in range(4)]
+
     x = boxes[...].reshape(devices, boxes.shape[2]).T[:coefs, :].astype(BF16)
     picked = dot(x, sel[:devices, :]).astype(BF16)
-    coarse = apply_eight(lambda c: up[c], picked).astype(BF16)
+    coarse = apply_eight(lambda c: up[c, :coefs, :], picked).astype(BF16)
+    add_kinds(turns[0])
     box = me // 8
     total = None
-    for j in range(csrc_ref.shape[0]):
-        hit = (iota((LANES, LANES), 0) == csrc_ref[j, box]) & (iota((LANES, LANES), 1) == 0)
+    for j in range(csrc_ref.shape[1]):
+        hit = (iota((LANES, LANES), 0) == csrc_ref[box, j]) & (iota((LANES, LANES), 1) == 0)
         picked = dot(coarse, hit.astype(F32).astype(BF16)).astype(BF16)
-        term = dot(farw[ckind_ref[j, box]], picked)
+        term = dot(farw[ckind_ref[box, j], :coefs, :], picked)
         total = term if total is None else total + term
     x = total.astype(BF16)
-
-    loads[3].wait()
-    x = dot(down[me % 8], x).astype(BF16)
+    add_kinds(turns[1])
+
+    x = dot(down[me % 8, :coefs, :], x).astype(BF16)
     for level in range(LOCAL_LEVELS - 1):
         picked = dot(x, spread[...]).astype(BF16)
-        x = apply_eight(lambda c: down[c], picked).astype(BF16)
+        x = apply_eight(lambda c: down[c, :coefs, :], picked).astype(BF16)
+        add_kinds(turns[2 + level])
     half = LANES // 2
     shape = (LANES, LANES)
     shift = ((iota(shape, 0) + half == iota(shape, 1)) & (iota(shape, 0) < half)).astype(F32)
     shifted = dot(x, shift.astype(BF16)).astype(BF16)
     result = far_total[...]
     for pair in range(4):
-        chain = dot(down[2 * pair], x) + dot(down[2 * pair + 1], shifted)
+        chain = dot(down[2 * pair, :coefs, :], x) + dot(down[2 * pair + 1, :coefs, :], shifted)
         upper = chain.astype(BF16)
         lower = (chain - upper.astype(F32)).astype(BF16)
         place = iota((LANES, leaves), 0)
@@ -253,11 +302,15 @@
     peers = sizes[1] * sizes[2]
     devices = sizes[0] * peers
 
+    def rows(table):
+        return table.transpose(1, 0, 2).reshape(-1, table.shape[2])
+
     def on_device(mult, up, down, farw, send, src, kind, csrc, ckind):
         coefs, leaves = mult.shape
         kinds = farw.shape[0]
         slots = send.shape[3]
         sources = leaves + peers * slots
+        tall = -(-coefs // 16) * 16
         wide = -(-coefs // LANES) * LANES
         vmem = pl.BlockSpec(memory_space=pltpu.VMEM)
         smem = pl.BlockSpec(memory_space=pltpu.SMEM)
@@ -269,9 +322,12 @@
             out_specs=vmem,
             scratch_shapes=[
                 pltpu.VMEM(mult.shape, BF16),
-                pltpu.VMEM(up.shape, BF16),
-                pltpu.VMEM(down.shape, BF16),
-                pltpu.VMEM(farw.shape, BF16),
+                pltpu.VMEM((8 * coefs, coefs), BF16),
+                pltpu.VMEM((8 * coefs, coefs), BF16),
+                pltpu.VMEM((8 * coefs, coefs), BF16),
+                pltpu.VMEM((8, tall, coefs), BF16),
+                pltpu.VMEM((8, tall, coefs), BF16),
+                pltpu.VMEM((8, tall, coefs), BF16),
                 pltpu.VMEM((leaves, 8 * LANES), BF16),
                 pltpu.VMEM((LANES, 8 * LANES), BF16),
                 pltpu.VMEM((peers * slots, wide), BF16),
@@ -291,7 +347,17 @@
             compiler_params=pltpu.CompilerParams(
                 collective_id=0, has_side_effects=True, vmem_limit_bytes=50 * 2**20
             ),
-        )(mult, up, down, farw, send.reshape(peers, slots), src, kind, csrc, ckind)
+        )(
+            mult,
+            rows(up),
+            rows(down),
+            rows(farw),
+            send.reshape(peers, slots),
+            src,
+            kind,
+            csrc.T,
+            ckind.T,
+        )
 
     leaf = P(None, ("gx", "gy", "gz"))
     in_specs = (leaf, P(), P(), P(), P("gx", ("gy", "gz"), None, None), leaf, leaf, P(), P())

time: 42.1 us -> 36.1 us (0.86)
  Pallas kernels: 34.2 us -> 29 us
  local copies, waits for them, and re-layouts: 7.68 us -> 6.73 us
    pallas_call x1, Pallas kernels: 34.2 us -> 29 us  [on_device(): pl.pallas_call(functools.partial(kernel, sizes), out_shape=jax.ShapeDtype...]
    unnamed x18 -> x15, local copies, waits for them, and re-layouts: 7.68 us -> 6.73 us
where the time goes in v2:
time: 36.1 us; the launch traced here: 35.7 us
  Pallas kernels  29 us (80%)
  local copies, waits for them, and re-layouts  6.73 us (19%)
    pallas_call x1, Pallas kernels, on_device(): pl.pallas_call(functools.partial(kernel, sizes), out_shape=jax.ShapeDtype...  29 us
    unnamed x15, local copies, waits for them, and re-layouts  6.73 us

profile of v2, /device:TPU:0, one launch (start us, length us, event | category | flops | bytes accessed | tf_op | source)
XLA Modules:
  0.0 35.7 jit_solution(4513821818339489728)
XLA Ops:
  0.0 0.0 copy-start
  0.0 1.5 %copy-done = bf16[8,289,289]{2,0,1:T(8,128)(2,1)S(1)} copy-done((bf16[8,289,289]{2,0,1:T(8,128)(2,1)S(1)}, bf16[8,289,289]{2,0,1:T(8,128)(2,1)}, u32[]{:S(2)}) %copy-start) | copy-done | bytes 1336360
  1.5 0.0 copy-start.1
  1.5 1.0 %copy-done.1 = bf16[289,512]{1,0:T(8,128)(2,1)S(1)} copy-done((bf16[289,512]{1,0:T(8,128)(2,1)S(1)}, bf16[289,512]{1,0:T(8,128)(2,1)}, u32[]{:S(2)}) %copy-start.1) | copy-done | bytes 295960
  2.4 0.0 copy-start.2
  2.4 0.8 %copy-done.2 = s32[16,512]{1,0:T(8,128)S(1)} copy-done((s32[16,512]{1,0:T(8,128)S(1)}, s32[16,512]{1,0:T(8,128)}, u32[]{:S(2)}) %copy-start.2) | copy-done | bytes 32792
  3.2 0.0 copy-start.3
  3.2 0.8 %copy-done.3 = s32[16,512]{1,0:T(8,128)S(1)} copy-done((s32[16,512]{1,0:T(8,128)S(1)}, s32[16,512]{1,0:T(8,128)}, u32[]{:S(2)}) %copy-start.3) | copy-done | bytes 32792
  4.0 0.0 copy-start.4
  4.0 0.7 %copy-done.4 = s32[1,1,16,16]{3,2,1,0:T(8,128)S(1)} copy-done((s32[1,1,16,16]{3,2,1,0:T(8,128)S(1)}, s32[1,1,16,16]{3,2,1,0:T(8,128)}, u32[]{:S(2)}) %copy-start.4) | copy-done | bytes 1048
  4.7 0.0 copy-start.5
  4.7 0.7 %copy-done.5 = s32[8,4]{0,1:T(4,128)S(1)} copy-done((s32[8,4]{0,1:T(4,128)S(1)}, s32[8,4]{0,1:T(4,128)}, u32[]{:S(2)}) %copy-start.5) | copy-done | bytes 152
  5.3 0.0 copy-start.6
  5.3 0.7 %copy-done.6 = s32[8,4]{0,1:T(4,128)S(1)} copy-done((s32[8,4]{0,1:T(4,128)S(1)}, s32[8,4]{0,1:T(4,128)}, u32[]{:S(2)}) %copy-start.6) | copy-done | bytes 152
  6.0 29.0 %shard_map.91 = bf16[289,512]{1,0:T(8,128)(2,1)S(1)} custom-call(bf16[289,512]{1,0:T(8,128)(2,1)S(1)} %copy-done.1, bf16[2312,289]{1,0:T(8,128)(2,1)S(1)} %bitcast.12, bf16[2312,289]{1,0:T(8,128)(2,1)} %bitcast.16, bf16[2312,289]{1,0:T(8,128)(2,1)} %bitcast.17, s32[16,16]{1,0:T(8,128)S(1)} %bitcast.13, s32[16,512]{1,0:T(8,128)S(1)} %copy-done.2, ...), custom_call_target="tpu_custom_call" | custom-call | tf_op jit(solution)/shard_map/pallas_call | solution.py:318
  35.0 0.7 %copy.11 = bf16[289,512]{1,0:T(8,128)(2,1)} copy(bf16[289,512]{1,0:T(8,128)(2,1)S(1)} %shard_map.91) | data formatting | bytes 591872
Async XLA Ops:
  0.0 1.5 %copy-start = (bf16[8,289,289]{2,0,1:T(8,128)(2,1)S(1)}, bf16[8,289,289]{2,0,1:T(8,128)(2,1)}, u32[]{:S(2)}) copy-start(bf16[8,289,289]{2,0,1:T(8,128)(2,1)} %param.10) | copy-start | bytes 4009012
  1.5 1.0 %copy-start.1 = (bf16[289,512]{1,0:T(8,128)(2,1)S(1)}, bf16[289,512]{1,0:T(8,128)(2,1)}, u32[]{:S(2)}) copy-start(bf16[289,512]{1,0:T(8,128)(2,1)} %mult_hbm.1) | copy-start | bytes 887812
  2.4 0.8 %copy-start.2 = (s32[16,512]{1,0:T(8,128)S(1)}, s32[16,512]{1,0:T(8,128)}, u32[]{:S(2)}) copy-start(s32[16,512]{1,0:T(8,128)} %src_ref.1) | copy-start | bytes 98308
  3.2 0.8 %copy-start.3 = (s32[16,512]{1,0:T(8,128)S(1)}, s32[16,512]{1,0:T(8,128)}, u32[]{:S(2)}) copy-start(s32[16,512]{1,0:T(8,128)} %kind_ref.1) | copy-start | bytes 98308
  4.0 0.7 %copy-start.4 = (s32[1,1,16,16]{3,2,1,0:T(8,128)S(1)}, s32[1,1,16,16]{3,2,1,0:T(8,128)}, u32[]{:S(2)}) copy-start(s32[1,1,16,16]{3,2,1,0:T(8,128)} %param.13) | copy-start | bytes 3076
  4.7 0.7 %copy-start.5 = (s32[8,4]{0,1:T(4,128)S(1)}, s32[8,4]{0,1:T(4,128)}, u32[]{:S(2)}) copy-start(s32[8,4]{0,1:T(4,128)} %param.16) | copy-start | bytes 388
  5.3 0.7 %copy-start.6 = (s32[8,4]{0,1:T(4,128)S(1)}, s32[8,4]{0,1:T(4,128)}, u32[]{:S(2)}) copy-start(s32[8,4]{0,1:T(4,128)} %param.17) | copy-start | bytes 388

commit v3 on v2

--- a/solution.py
+++ b/solution.py
@@ -40,10 +40,17 @@
     return hit.astype(F32).astype(BF16)
 
 
+def stack_two(first, second, depth):
+    gap = jnp.zeros((depth // 2 - first.shape[0], first.shape[1]), BF16)
+    return jnp.concatenate([first, gap, second, gap], axis=0)
+
+
 def apply_eight(table, blocks):
     total = None
-    for c in range(8):
-        term = dot(table(c), blocks[:, c * LANES : (c + 1) * LANES])
+    for pair in range(4):
+        first = blocks[:, 2 * pair * LANES : (2 * pair + 1) * LANES]
+        second = blocks[:, (2 * pair + 1) * LANES : (2 * pair + 2) * LANES]
+        term = dot(table[pair], stack_two(first, second, table.shape[2]))
         total = term if total is None else total + term
     return total
 
@@ -56,7 +63,8 @@
     out = dot(order, rows).astype(BF16)
     for c in range(8):
         spot = pl.ds(pl.multiple_of(step * BLOCK, BLOCK), BLOCK)
-        table[c, spot, :] = out[c * BLOCK : (c + 1) * BLOCK]
+        at = c % 2 * (table.shape[2] // 2)
+        table[c // 2, spot, at : at + out.shape[1]] = out[c * BLOCK : (c + 1) * BLOCK]
 
 
 def split_tail(raw, table):
@@ -69,7 +77,8 @@
     hit = (frm == 8 * (to % room) + to // room) & (to % room < left)
     out = dot(hit.astype(F32).astype(BF16), raw[8 * done :, :]).astype(BF16)
     for c in range(8):
-        table[c, done:, :] = out[c * room : (c + 1) * room]
+        at = c % 2 * (table.shape[2] // 2)
+        table[c // 2, done:, at : at + out.shape[1]] = out[c * room : (c + 1) * room]
 
 
 def kernel(
@@ -78,12 +87,17 @@
     up_hbm,
     down_hbm,
     far_hbm,
+    send_hbm,
+    src_hbm,
+    kind_hbm,
+    csrc_hbm,
+    ckind_hbm,
+    out_ref,
     send_ref,
     src_ref,
     kind_ref,
     csrc_ref,
     ckind_ref,
-    out_ref,
     mult,
     up_raw,
     down_raw,
@@ -99,6 +113,7 @@
     buf,
     far_total,
     turn,
+    coarse_hot,
     message,
     boxes,
     load_sem,
@@ -115,14 +130,24 @@
     me = gx * peers + q
     coefs, leaves = mult.shape
     slots = send_ref.shape[1]
-    kinds = farw.shape[0]
+    kinds = table.shape[0]
     sources = table.shape[1]
     list_len = src_ref.shape[0]
 
     loads = [
         pltpu.make_async_copy(a, b, load_sem.at[i])
         for i, (a, b) in enumerate(
-            ((up_hbm, up_raw), (mult_hbm, mult), (far_hbm, far_raw), (down_hbm, down_raw))
+            (
+                (up_hbm, up_raw),
+                (mult_hbm, mult),
+                (send_hbm, send_ref),
+                (src_hbm, src_ref),
+                (kind_hbm, kind_ref),
+                (csrc_hbm, csrc_ref),
+                (ckind_hbm, ckind_ref),
+                (far_hbm, far_raw),
+                (down_hbm, down_raw),
+            )
         )
     ]
     for load in loads:
@@ -144,6 +169,11 @@
     sel[...] = pick_children(leaves)
     spread[...] = spread_children()
     blocks = coefs // BLOCK
+    half_depth = up.shape[2] // 2
+    for one in (up, farw, down):
+        for end in (half_depth, 2 * half_depth):
+            one[:, :, end - LANES : end] = jnp.zeros(one.shape[:2] + (LANES,), BF16)
+    buf[...] = jnp.zeros_like(buf)
     loads[0].wait()
 
     def split_up(i, carry):
@@ -154,16 +184,18 @@
     split_tail(up_raw, up)
     loads[1].wait()
     turn[...] = jnp.zeros_like(turn)
-    x = mult[...]
+    buf[:coefs, :leaves] = mult[...]
+    x = buf[:, :leaves]
     for level in range(LOCAL_LEVELS):
         picked = dot(x, sel[: x.shape[1], :]).astype(BF16)
-        total = apply_eight(lambda c: up[c, :coefs, :], picked)
+        total = apply_eight(up, picked)
         x = total.astype(BF16)
-    turn[:coefs, :] = x.astype(F32)
+    turn[: x.shape[0], :] = x.astype(F32)
     row = turn[...].T[0:1, :]
     message[...] = row
     boxes[me] = row
 
+    loads[2].wait()
     count = peers * slots
     row_of = (iota((count, peers), 0) // slots == iota((count, peers), 1)).astype(F32).astype(BF16)
     wanted = send_ref[...]
@@ -233,8 +265,8 @@
         split_octants(down_raw, down, step)
         return count_rows(step, carry)
 
-    loads[2].wait()
-    loads[3].wait()
+    for load in loads[3:]:
+        load.wait()
     both = min(blocks, sources // ROWS)
     assert both == blocks
     lax.fori_loop(0, both, count_and_split, 0)
@@ -242,54 +274,62 @@
     split_tail(far_raw, farw)
     split_tail(down_raw, down)
 
-    buf[:, :leaves] = mult[...]
+    box = me // 8
+    total = jnp.zeros(coarse_hot.shape, jnp.int32)
+    for j in range(csrc_ref.shape[1]):
+        hit = (iota(total.shape, 0) == csrc_ref[box, j]) & (
+            iota(total.shape, 1) == ckind_ref[box, j] * LANES
+        )
+        total = total + jnp.where(hit, 1, 0)
+    coarse_hot[...] = total.astype(F32).astype(BF16)
+
     part = arrived.at[pl.ds(0, (peers - 1) * slots)]
     pltpu.make_async_copy(part, part, a2a_recv).wait()
-    buf[:, leaves:] = arrived[...].astype(F32).T[:coefs, :].astype(BF16)
+    buf[:coefs, leaves:] = arrived[...].astype(F32).T[:coefs, :].astype(BF16)
     part = boxes.at[pl.ds(0, devices - 1)]
     pltpu.make_async_copy(part, part, box_recv).wait()
     far_total[...] = jnp.zeros_like(far_total)
 
     def add_kinds(which):
-        for k in which:
-            grouped = dot(buf[...], table[k]).astype(BF16)
-            far_total[...] += dot(farw[k, :coefs, :], grouped)
-
-    turns = [range(t * kinds // 4, (t + 1) * kinds // 4) for t in range(4)]
-
-    x = boxes[...].reshape(devices, boxes.shape[2]).T[:coefs, :].astype(BF16)
+        for pair in which:
+            first = dot(buf[...], table[2 * pair]).astype(BF16)
+            second = dot(buf[...], table[2 * pair + 1]).astype(BF16)
+            far_total[...] += dot(farw[pair], stack_two(first, second, farw.shape[2]))
+
+    turns = [range(t * kinds // 8, (t + 1) * kinds // 8) for t in range(4)]
+
+    x = boxes[...].reshape(devices, boxes.shape[2]).T[: buf.shape[0], :].astype(BF16)
     picked = dot(x, sel[:devices, :]).astype(BF16)
-    coarse = apply_eight(lambda c: up[c, :coefs, :], picked).astype(BF16)
+    coarse = apply_eight(up, picked).astype(BF16)
     add_kinds(turns[0])
-    box = me // 8
-    total = None
-    for j in range(csrc_ref.shape[1]):
-        hit = (iota((LANES, LANES), 0) == csrc_ref[box, j]) & (iota((LANES, LANES), 1) == 0)
-        picked = dot(coarse, hit.astype(F32).astype(BF16)).astype(BF16)
-        term = dot(farw[ckind_ref[box, j], :coefs, :], picked)
-        total = term if total is None else total + term
-    x = total.astype(BF16)
+    picked = dot(coarse, coarse_hot[...]).astype(BF16)
+    x = apply_eight(farw, picked).astype(BF16)
     add_kinds(turns[1])
 
-    x = dot(down[me % 8, :coefs, :], x).astype(BF16)
+    octant = me % 8
+    none = jnp.zeros_like(x)
+    is_odd = octant % 2 == 1
+    both = stack_two(jnp.where(is_odd, none, x), jnp.where(is_odd, x, none), down.shape[2])
+    x = dot(down[octant // 2], both).astype(BF16)
     for level in range(LOCAL_LEVELS - 1):
         picked = dot(x, spread[...]).astype(BF16)
-        x = apply_eight(lambda c: down[c, :coefs, :], picked).astype(BF16)
+        x = apply_eight(down, picked).astype(BF16)
         add_kinds(turns[2 + level])
     half = LANES // 2
     shape = (LANES, LANES)
     shift = ((iota(shape, 0) + half == iota(shape, 1)) & (iota(shape, 0) < half)).astype(F32)
     shifted = dot(x, shift.astype(BF16)).astype(BF16)
     result = far_total[...]
+    both = stack_two(x, shifted, down.shape[2])
     for pair in range(4):
-        chain = dot(down[2 * pair, :coefs, :], x) + dot(down[2 * pair + 1, :coefs, :], shifted)
+        chain = dot(down[pair], both)
         upper = chain.astype(BF16)
         lower = (chain - upper.astype(F32)).astype(BF16)
-        place = iota((LANES, leaves), 0)
+        place = iota((2 * LANES, leaves), 0) % LANES
         goes = 8 * (place % half) + place // half + 2 * pair
-        spot = (goes == iota((LANES, leaves), 1)).astype(F32).astype(BF16)
-        result = result + dot(upper, spot) + dot(lower, spot)
-    out_ref[...] = result.astype(BF16)
+        spot = (goes == iota((2 * LANES, leaves), 1)).astype(F32).astype(BF16)
+        result = result + dot(jnp.concatenate([upper, lower], axis=1), spot)
+    out_ref[...] = result[:coefs].astype(BF16)
 
     part = out_rows.at[pl.ds(0, (peers - 1) * slots)]
     pltpu.make_async_copy(part, part, a2a_send).wait()
@@ -313,39 +353,44 @@
         tall = -(-coefs // 16) * 16
         wide = -(-coefs // LANES) * LANES
         vmem = pl.BlockSpec(memory_space=pltpu.VMEM)
-        smem = pl.BlockSpec(memory_space=pltpu.SMEM)
         hbm = pl.BlockSpec(memory_space=pl.ANY)
         return pl.pallas_call(
             functools.partial(kernel, sizes),
             out_shape=jax.ShapeDtypeStruct((coefs, leaves), BF16),
-            in_specs=[hbm] * 4 + [vmem] * 3 + [smem] * 2,
+            in_specs=[hbm] * 9,
             out_specs=vmem,
             scratch_shapes=[
+                pltpu.VMEM((peers, slots), jnp.int32),
+                pltpu.VMEM(src.shape, jnp.int32),
+                pltpu.VMEM(kind.shape, jnp.int32),
+                pltpu.SMEM(csrc.shape[::-1], jnp.int32),
+                pltpu.SMEM(ckind.shape[::-1], jnp.int32),
                 pltpu.VMEM(mult.shape, BF16),
                 pltpu.VMEM((8 * coefs, coefs), BF16),
                 pltpu.VMEM((8 * coefs, coefs), BF16),
                 pltpu.VMEM((8 * coefs, coefs), BF16),
-                pltpu.VMEM((8, tall, coefs), BF16),
-                pltpu.VMEM((8, tall, coefs), BF16),
-                pltpu.VMEM((8, tall, coefs), BF16),
+                pltpu.VMEM((4, tall, 2 * wide), BF16),
+                pltpu.VMEM((4, tall, 2 * wide), BF16),
+                pltpu.VMEM((4, tall, 2 * wide), BF16),
                 pltpu.VMEM((leaves, 8 * LANES), BF16),
                 pltpu.VMEM((LANES, 8 * LANES), BF16),
                 pltpu.VMEM((peers * slots, wide), BF16),
                 pltpu.VMEM((peers * slots, wide), BF16),
                 pltpu.VMEM((kinds, sources, leaves), BF16),
-                pltpu.VMEM((coefs, sources), BF16),
-                pltpu.VMEM((coefs, leaves), F32),
+                pltpu.VMEM((tall, sources), BF16),
+                pltpu.VMEM((tall, leaves), F32),
                 pltpu.VMEM((wide, LANES), F32),
+                pltpu.VMEM((LANES, 8 * LANES), BF16),
                 pltpu.VMEM((1, wide), F32),
                 pltpu.VMEM((devices, 1, wide), F32),
-                pltpu.SemaphoreType.DMA((4,)),
+                pltpu.SemaphoreType.DMA((9,)),
                 pltpu.SemaphoreType.DMA,
                 pltpu.SemaphoreType.DMA,
                 pltpu.SemaphoreType.DMA,
                 pltpu.SemaphoreType.DMA,
             ],
             compiler_params=pltpu.CompilerParams(
-                collective_id=0, has_side_effects=True, vmem_limit_bytes=50 * 2**20
+                collective_id=0, has_side_effects=True, vmem_limit_bytes=63 * 2**20
             ),
         )(
             mult,

time: 36.1 us -> 29.6 us (0.82)
  local copies, waits for them, and re-layouts: 6.73 us -> 1.7 us
  Pallas kernels: 29 us -> 27.7 us
    unnamed x15 -> x1, local copies, waits for them, and re-layouts: 6.73 us -> 1.7 us
    pallas_call x1, Pallas kernels: 29 us -> 27.7 us  [on_device(): pl.pallas_call(functools.partial(kernel, sizes), out_shape=jax.ShapeDtype...]
where the time goes in v3:
time: 29.6 us; the launch traced here: 29.4 us
  Pallas kernels  27.7 us (94%)
  local copies, waits for them, and re-layouts  1.7 us (6%)
    pallas_call x1, Pallas kernels, on_device(): pl.pallas_call(functools.partial(kernel, sizes), out_shape=jax.ShapeDtype...  27.7 us
    unnamed x1, local copies, waits for them, and re-layouts  1.7 us

profile of v3, /device:TPU:0, one launch (start us, length us, event | category | flops | bytes accessed | tf_op | source)
XLA Modules:
  0.0 29.4 jit_solution(18364665138269148449)
XLA Ops:
  0.0 27.7 %shard_map.91 = bf16[289,512]{1,0:T(8,128)(2,1)} custom-call(bf16[289,512]{1,0:T(8,128)(2,1)} %mult_hbm.1, bf16[2312,289]{1,0:T(8,128)(2,1)} %bitcast.12, bf16[2312,289]{1,0:T(8,128)(2,1)} %bitcast.13, bf16[2312,289]{1,0:T(8,128)(2,1)} %bitcast.14, s32[16,16]{1,0:T(8,128)} %bitcast.15, s32[16,512]{1,0:T(8,128)} %src_hbm.1, s32[16,512]{1,0:T(8,128)} %kind_hbm.1, ...), custom_call_target="tpu_custom_call" | custom-call | tf_op jit(solution)/shard_map/pallas_call | solution.py:357
  27.7 1.7 %copy.11 = bf16[289,512]{1,0:T(8,128)(2,1)} copy(bf16[289,512]{1,0:T(8,128)(2,1)} %shard_map.91) | data formatting | bytes 591872

commit v4 on v3

--- a/solution.py
+++ b/solution.py
@@ -27,17 +27,16 @@
 
 
 def pick_children(rows):
-    shape = (rows, 8 * LANES)
-    col = iota(shape, 1)
-    return (iota(shape, 0) == 8 * (col % LANES) + col // LANES).astype(F32).astype(BF16)
+    col = iota((1, 8 * LANES), 1)
+    takes = 8 * (col % LANES) + col // LANES
+    return (iota((rows, 8 * LANES), 0) == takes).astype(F32).astype(BF16)
 
 
 def spread_children():
-    shape = (LANES, 8 * LANES)
-    col = iota(shape, 1)
+    col = iota((1, 8 * LANES), 1)
     place = col % LANES
-    hit = (iota(shape, 0) == place // 8) & (place % 8 == col // LANES)
-    return hit.astype(F32).astype(BF16)
+    takes = jnp.where(place % 8 == col // LANES, place // 8, -1)
+    return (iota((LANES, 8 * LANES), 0) == takes).astype(F32).astype(BF16)
 
 
 def stack_two(first, second, depth):
@@ -55,12 +54,15 @@
     return total
 
 
-def split_octants(raw, table, step):
-    shape = (8 * BLOCK, 8 * BLOCK)
-    to, frm = iota(shape, 0), iota(shape, 1)
-    order = (frm == 8 * (to % BLOCK) + to // BLOCK).astype(F32).astype(BF16)
+def octant_order():
+    to = iota((8 * BLOCK, 1), 0)
+    takes = 8 * (to % BLOCK) + to // BLOCK
+    return (iota((8 * BLOCK, 8 * BLOCK), 1) == takes).astype(F32).astype(BF16)
+
+
+def split_octants(raw, table, order, step):
     rows = raw[pl.ds(pl.multiple_of(step * 8 * BLOCK, 8 * BLOCK), 8 * BLOCK), :]
-    out = dot(order, rows).astype(BF16)
+    out = dot(order[...], rows).astype(BF16)
     for c in range(8):
         spot = pl.ds(pl.multiple_of(step * BLOCK, BLOCK), BLOCK)
         at = c % 2 * (table.shape[2] // 2)
@@ -114,6 +116,7 @@
     far_total,
     turn,
     coarse_hot,
+    order,
     message,
     boxes,
     load_sem,
@@ -166,6 +169,7 @@
 
     lax.fori_loop(1, devices, greet, 0)
 
+    order[...] = octant_order()
     sel[...] = pick_children(leaves)
     spread[...] = spread_children()
     blocks = coefs // BLOCK
@@ -177,7 +181,7 @@
     loads[0].wait()
 
     def split_up(i, carry):
-        split_octants(up_raw, up, i)
+        split_octants(up_raw, up, order, i)
         return carry
 
     lax.fori_loop(0, blocks, split_up, 0)
@@ -249,24 +253,26 @@
             for start in range(0, list_len, FIELD):
                 acc = jnp.zeros((ROWS, LANES), jnp.int32)
                 for j in range(start, min(start + FIELD, list_len)):
-                    weight = lax.shift_left(jnp.int32(1), 4 * kind_ref[j : j + 1, cols])
+                    weight = kind_ref[j : j + 1, cols]
                     acc = acc + jnp.where(src_ref[j : j + 1, cols] == sid, weight, 0)
                 parts.append(acc)
             even = sum(a & LOW_NIBBLES for a in parts)
             odd = sum(lax.shift_right_logical(a, 4) & LOW_NIBBLES for a in parts)
             for k in range(kinds):
                 word = odd if k % 2 else even
-                field = lax.shift_right_logical(word, 8 * (k // 2)) & 255
+                field = lax.shift_right_logical(word, 8 * (k // 2)) if k > 1 else word
+                field = field & 255 if k < 6 else field
                 table[k, pl.ds(s0, ROWS), cols] = field.astype(F32).astype(BF16)
         return carry
 
     def count_and_split(step, carry):
-        split_octants(far_raw, farw, step)
-        split_octants(down_raw, down, step)
+        split_octants(far_raw, farw, order, step)
+        split_octants(down_raw, down, order, step)
         return count_rows(step, carry)
 
     for load in loads[3:]:
         load.wait()
+    kind_ref[...] = lax.shift_left(jnp.int32(1), 4 * kind_ref[...])
     both = min(blocks, sources // ROWS)
     assert both == blocks
     lax.fori_loop(0, both, count_and_split, 0)
@@ -325,7 +331,7 @@
         chain = dot(down[pair], both)
         upper = chain.astype(BF16)
         lower = (chain - upper.astype(F32)).astype(BF16)
-        place = iota((2 * LANES, leaves), 0) % LANES
+        place = iota((2 * LANES, 1), 0) % LANES
         goes = 8 * (place % half) + place // half + 2 * pair
         spot = (goes == iota((2 * LANES, leaves), 1)).astype(F32).astype(BF16)
         result = result + dot(jnp.concatenate([upper, lower], axis=1), spot)
@@ -381,6 +387,7 @@
                 pltpu.VMEM((tall, leaves), F32),
                 pltpu.VMEM((wide, LANES), F32),
                 pltpu.VMEM((LANES, 8 * LANES), BF16),
+                pltpu.VMEM((8 * BLOCK, 8 * BLOCK), BF16),
                 pltpu.VMEM((1, wide), F32),
                 pltpu.VMEM((devices, 1, wide), F32),
                 pltpu.SemaphoreType.DMA((9,)),

time: 29.6 us -> 29.5 us (level)
  no operation moved by 1% of the time
where the time goes in v4:
time: 29.5 us; the launch traced here: 29.4 us
  Pallas kernels  27.7 us (94%)
  local copies, waits for them, and re-layouts  1.7 us (6%)
    pallas_call x1, Pallas kernels, on_device(): pl.pallas_call(functools.partial(kernel, sizes), out_shape=jax.ShapeDtype...  27.7 us
    unnamed x1, local copies, waits for them, and re-layouts  1.7 us

profile of v4, /device:TPU:0, one launch (start us, length us, event | category | flops | bytes accessed | tf_op | source)
XLA Modules:
  0.0 29.4 jit_solution(15931124111401103637)
XLA Ops:
  0.0 27.7 %shard_map.91 = bf16[289,512]{1,0:T(8,128)(2,1)} custom-call(bf16[289,512]{1,0:T(8,128)(2,1)} %mult_hbm.1, bf16[2312,289]{1,0:T(8,128)(2,1)} %bitcast.12, bf16[2312,289]{1,0:T(8,128)(2,1)} %bitcast.13, bf16[2312,289]{1,0:T(8,128)(2,1)} %bitcast.14, s32[16,16]{1,0:T(8,128)} %bitcast.15, s32[16,512]{1,0:T(8,128)} %src_hbm.1, s32[16,512]{1,0:T(8,128)} %kind_hbm.1, ...), custom_call_target="tpu_custom_call" | custom-call | tf_op jit(solution)/shard_map/pallas_call | solution.py:363
  27.7 1.7 %copy.11 = bf16[289,512]{1,0:T(8,128)(2,1)} copy(bf16[289,512]{1,0:T(8,128)(2,1)} %shard_map.91) | data formatting | bytes 591872
